TPU v7x, 256 devices: a whole 4x4x8 slice. The times are simulated.
256 devices in a mesh: sub: 2 (over y_lo), col: 32 (over z, y_hi, core), row: 4 (over x).
Axes of the slice: x: 4, y: 4 (y_hi: 2, y_lo: 2; y = y_hi * 2 + y_lo), z: 8, core: 2. Of those that a mesh axis runs over, the one named last changes fastest.
Arguments:
- front_in: float32 [16384, 16384], P(('sub', 'row'), 'col'), as said below
- child_update: float32 [2, 8192, 8192], P('sub', 'row', 'col'), as said below
- child_map: int32 [2, 8192], replicated, may hold values from 0 to 16383, as said below
Outputs:
- front_out: float32 [16384, 16384], P(('sub', 'row'), 'col')
Inputs may be any that keep to these rules, and one draw needn't show every extreme that they name: `child_map`: for each child c the map is one to one; it takes the 256 indices of child tile t onto all 256 indices of one parent tile whose number is congruent to t modulo 32. The two children may land on the same parent tiles. `front_in`: in natural order the front is symmetric, each child's update is symmetric, and the assembled front is positive definite. `child_update`: in natural order each child's update is symmetric.
All inputs are finite; a program needn't handle non-finite values.
Results may differ from a plain program's by a relative error of at most 0.0001.
Values sent between devices are 32-bit elements; how exact they have to be, the bound alone decides.
A program may use at most 64 MiB of HBM per device.

v0:
```python
import jax
import jax.numpy as jnp
from jax import lax
from jax.sharding import PartitionSpec as P

TILE_SIZE = 256
PANELS = 2


def from_root(x, axis, root):
    mine = lax.axis_index(axis) == root
    return lax.psum(jnp.where(mine, x, jnp.zeros_like(x)), axis)


def product_nt(left, right):
    return lax.dot_general(left, right, (((1,), (1,)), ((), ())), precision=lax.Precision.HIGHEST)


def product_nn(left, right):
    return lax.dot_general(left, right, (((1,), (0,)), ((), ())), precision=lax.Precision.HIGHEST)


def factorize(corner):
    order_now = corner.shape[0]
    if order_now <= 32:
        factor = jnp.linalg.cholesky(corner)
        inverse = lax.linalg.triangular_solve(
            factor, jnp.eye(order_now, dtype=jnp.float32), left_side=True, lower=True
        )
        return (factor, inverse)
    half = order_now // 2
    upper_factor, upper_inverse = factorize(corner[:half, :half])
    below = product_nt(corner[half:, :half], upper_inverse)
    schur = corner[half:, half:] - product_nt(below, below)
    lower_factor, lower_inverse = factorize(schur)
    mixed = -product_nn(product_nn(lower_inverse, below), upper_inverse)
    zeros_block = jnp.zeros((half, order_now - half), jnp.float32)
    factor = jnp.concatenate(
        [
            jnp.concatenate([upper_factor, zeros_block], 1),
            jnp.concatenate([below, lower_factor], 1),
        ],
        0,
    )
    inverse = jnp.concatenate(
        [
            jnp.concatenate([upper_inverse, zeros_block], 1),
            jnp.concatenate([mixed, lower_inverse], 1),
        ],
        0,
    )
    return (factor, inverse)


def finish(source_data, factor, inverse, tile_ids, number, contract):
    product = lax.dot_general(
        source_data, inverse, (contract, ((), ())), precision=lax.Precision.HIGHEST
    )
    tiled_factor = jnp.tile(factor, (product.shape[0] // factor.shape[0], 1))
    return jnp.where(
        (tile_ids < number)[:, None],
        0.0,
        jnp.where((tile_ids == number)[:, None], tiled_factor, product),
    )


def local(front_in, child_update, child_map):
    sub_count = lax.axis_size("sub")
    row_count = lax.axis_size("row")
    col_count = lax.axis_size("col")
    group_count = sub_count * row_count
    my_group = lax.axis_index("sub") * row_count + lax.axis_index("row")
    my_column = lax.axis_index("col")
    tile_width = TILE_SIZE
    row_local, col_local = front_in.shape
    child_rows = child_update.shape[1]
    child_cols = child_update.shape[2]
    blocks = child_rows // tile_width // sub_count
    pieces = child_update[0].reshape(blocks, sub_count, tile_width, child_cols)
    arrived = lax.all_to_all(pieces, "sub", split_axis=1, concat_axis=1, tiled=True)
    offsets = jnp.arange(tile_width, dtype=jnp.int32)
    child_row_index = (
        (jnp.arange(blocks, dtype=jnp.int32)[:, None] * group_count + my_group) * tile_width
        + offsets[None, :]
    ).reshape(-1)
    child_col_index = (
        (jnp.arange(child_cols // tile_width, dtype=jnp.int32)[:, None] * col_count + my_column)
        * tile_width
        + offsets[None, :]
    ).reshape(-1)
    front = front_in
    for source in range(sub_count):
        parent_rows = jnp.take(child_map[source], child_row_index)
        parent_cols = jnp.take(child_map[source], child_col_index)
        local_rows = (
            parent_rows // tile_width // group_count * tile_width + parent_rows % tile_width
        )
        local_cols = parent_cols // tile_width // col_count * tile_width + parent_cols % tile_width
        row_pick = (
            jnp.full((row_local,), -1, jnp.int32)
            .at[local_rows]
            .set(jnp.arange(local_rows.shape[0], dtype=jnp.int32))
        )
        col_pick = (
            jnp.full((col_local,), -1, jnp.int32)
            .at[local_cols]
            .set(jnp.arange(local_cols.shape[0], dtype=jnp.int32))
        )
        incoming = arrived[:, source].reshape(-1, child_cols)
        gathered = jnp.take(
            jnp.take(incoming, jnp.maximum(row_pick, 0), axis=0), jnp.maximum(col_pick, 0), axis=1
        )
        present = jnp.logical_and((row_pick >= 0)[:, None], (col_pick >= 0)[None, :])
        front = front + jnp.where(present, gathered, 0.0)
    row_tiles = jnp.repeat(
        jnp.arange(row_local // tile_width, dtype=jnp.int32) * group_count + my_group, tile_width
    )
    col_tiles = jnp.repeat(
        jnp.arange(col_local // tile_width, dtype=jnp.int32) * col_count + my_column, tile_width
    )
    for number in range(PANELS):
        owner = number % col_count
        local_tile = number // col_count
        diag_group = number % group_count
        diag_tile = number // group_count
        own_column = front[:, local_tile * tile_width : (local_tile + 1) * tile_width]
        column = from_root(own_column, "col", owner)
        corner = from_root(
            column[diag_tile * tile_width : (diag_tile + 1) * tile_width],
            ("sub", "row"),
            diag_group,
        )
        factor, inverse = factorize(corner)
        left_rows = finish(column, factor, inverse, row_tiles, number, ((1,), (1,)))
        shared = min(col_count, group_count)
        spread = max(col_count // group_count, 1)
        shaped = left_rows.reshape(
            row_local // tile_width // spread, spread, tile_width, tile_width
        )
        pick = (my_column - my_group) // group_count % spread
        chosen = lax.dynamic_index_in_dim(shaped, pick, 1, keepdims=False)
        arrivals = [from_root(chosen, ("sub", "row"), my_column % shared + shared * 0)]
        right_rows = jnp.stack(arrivals, 1).reshape(col_local, tile_width)
        update = lax.dot_general(
            left_rows, right_rows, (((1,), (1,)), ((), ())), precision=lax.Precision.HIGHEST
        )
        later_rows = (row_tiles > number)[:, None]
        later_cols = (col_tiles > number)[None, :]
        at_panel = (col_tiles == number)[None, :]
        filled = jnp.tile(left_rows, (1, col_local // tile_width))
        front = jnp.where(
            later_cols,
            jnp.where(later_rows, front - update, 0.0),
            jnp.where(at_panel, filled, front),
        )
    return front


def solution(mesh):
    placed = (P(("sub", "row"), "col"), P("sub", "row", "col"), P())
    return jax.shard_map(
        local, mesh=mesh, in_specs=placed, out_specs=P(("sub", "row"), "col"), check_vma=False
    )
```

profile of v0, /device:TPU:60, one launch (start us, length us, event | category | flops | bytes accessed | tf_op | source)
XLA Modules:
  0.0 1155.5 jit_solution(16723078077921959594)
XLA Ops:
  6.5 3.0 copy.47
  9.6 5.7 all-to-all-start
  15.4 6.2 gather_fusion
  21.6 6.2 gather_fusion.4
  34.2 5.3 copy.49
  39.5 4.3 scatter_custom_fusion.2
  43.9 4.8 scatter_custom_fusion
  50.6 8.6 gather_fusion.6
  59.1 3.3 broadcast_select_fusion
  64.3 8.6 gather_fusion.2
  72.9 3.3 broadcast_select_fusion.1
  76.2 3.0 copy.48
  79.1 3.6 gather_fusion.7
  82.7 7.0 gather_fusion.3
  89.7 5.7 fusion.2
  98.9 267.6 %all-reduce.35.cloned.1.call-done = f32[2048,256]{0,1:T(8,128)} async-done(((f32[2048,256]{0,1:T(8,128)}), f32[2048,256]{0,1:T(8,128)}) %all-reduce.35.cloned.1.call-update) | async-done | bytes 2097168 | tf_op jit(solution)/shard_map/psum | solution.py:12
  368.7 85.2 %all-reduce.37.cloned.1.call-done = f32[256,256]{0,1:T(8,128)} async-done(((f32[256,256]{0,1:T(8,128)}), f32[256,256]{0,1:T(8,128)}) %all-reduce.37.cloned.1.call-update) | async-done | bytes 262160 | tf_op jit(solution)/shard_map/psum | solution.py:12
  480.9 2.9 cholesky.287
  498.2 2.9 cholesky.309
  513.7 2.9 cholesky.331
  528.9 3.4 fusion.6
  533.5 79.4 %all-reduce.39.cloned.1.call-done = f32[512,256]{0,1:T(8,128)} async-done(((f32[512,256]{0,1:T(8,128)}), f32[512,256]{0,1:T(8,128)}) %all-reduce.39.cloned.1.call-update) | async-done | bytes 524304 | tf_op jit(solution)/shard_map/psum | solution.py:12
  612.9 6.1 fusion.1
  622.6 266.8 %all-reduce.41.cloned.1.call-done = f32[2048,256]{0,1:T(8,128)} async-done(((f32[2048,256]{0,1:T(8,128)}), f32[2048,256]{0,1:T(8,128)}) %all-reduce.41.cloned.1.call-update) | async-done | bytes 2097168 | tf_op jit(solution)/shard_map/psum | solution.py:12
  891.3 85.1 %all-reduce.43.cloned.1.call-done = f32[256,256]{0,1:T(8,128)} async-done(((f32[256,256]{0,1:T(8,128)}), f32[256,256]{0,1:T(8,128)}) %all-reduce.43.cloned.1.call-update) | async-done | bytes 262160 | tf_op jit(solution)/shard_map/psum | solution.py:12
  1003.4 2.9 cholesky.375
  1020.8 2.9 cholesky.397
  1036.2 2.9 cholesky.419
  1051.5 3.4 fusion.7
  1056.0 79.5 %all-reduce.45.cloned.1.call-done = f32[512,256]{0,1:T(8,128)} async-done(((f32[512,256]{0,1:T(8,128)}), f32[512,256]{0,1:T(8,128)}) %all-reduce.45.cloned.1.call-update) | async-done | bytes 524304 | tf_op jit(solution)/shard_map/psum | solution.py:12
  1135.5 7.4 fusion
  1142.9 5.3 copy.89
  (302 shorter events, 155.3 us)
Async XLA Ops:
  9.6 5.8 copy-start.4
  9.6 39.2 %all-to-all-start = ((f32[4,2,256,256]{3,2,0,1:T(8,128)}), f32[4,2,256,256]{3,2,0,1:T(8,128)}, u32[]{:S(2)}, u32[]{:S(2)}) async-start(f32[4,2,256,256]{3,2,0,1:T(8,128)} %copy.47), calls=%async_computation | async-start | bytes 4194304 | tf_op jit(solution)/shard_map/all_to_all | solution.py:80
  15.2 351.3 %all-reduce.35.cloned.1.call-start = ((), (), s32[]{:S(2)}) async-start(), calls=%async_computation.1 | async-start | bytes 4194304 | tf_op jit(solution)/shard_map/psum | solution.py:12
  95.4 2.0 copy-start
  98.9 355.0 %all-reduce.37.cloned.1.call-start = ((), (), s32[]{:S(2)}) async-start(), calls=%async_computation.2 | async-start | bytes 524288 | tf_op jit(solution)/shard_map/psum | solution.py:12
  368.2 244.7 %all-reduce.39.cloned.1.call-start = ((), (), s32[]{:S(2)}) async-start(), calls=%async_computation.3 | async-start | bytes 1048576 | tf_op jit(solution)/shard_map/psum | solution.py:12
  522.4 1.6 copy-start.2
  533.2 356.2 %all-reduce.41.cloned.1.call-start = ((), (), s32[]{:S(2)}) async-start(), calls=%async_computation.4 | async-start | bytes 4194304 | tf_op jit(solution)/shard_map/psum | solution.py:12
  619.0 2.0 copy-start.1
  622.5 353.9 %all-reduce.43.cloned.1.call-start = ((), (), s32[]{:S(2)}) async-start(), calls=%async_computation.5 | async-start | bytes 524288 | tf_op jit(solution)/shard_map/psum | solution.py:12
  891.1 244.4 %all-reduce.45.cloned.1.call-start = ((), (), s32[]{:S(2)}) async-start(), calls=%async_computation.6 | async-start | bytes 1048576 | tf_op jit(solution)/shard_map/psum | solution.py:12
  1044.9 1.6 copy-start.3
Sparse Core Ops, SparseCore 0:
  99.0 267.4 all-reduce.34
  369.3 84.5 all-reduce.36
  533.3 79.5 all-reduce.38
  622.7 266.6 all-reduce.40
  891.9 84.5 all-reduce.42
  1055.9 79.5 all-reduce.44
where the time goes:
time: 1160 us
  waiting for transfers between devices  864 us (74%)
  other arithmetic  134 us (12%)
  local copies, waits for them, and re-layouts  94.4 us (8%)
  matrix products  42 us (4%)
  between operations  15.2 us (1%)
    psum x6, waiting for transfers between devices, from_root(): return lax.psum(jnp.where(mine, x, jnp.zeros_like(x)), axis)  863 us
    another operation x48, other arithmetic, factorize(): factor = jnp.linalg.cholesky(corner)  57.5 us
    another operation x32, other arithmetic, factorize(): lax.linalg.triangular_solve(factor, jnp.eye(order_now, dtype=jnp.float32)...  48.4 us
  transfers between devices with their start and end apart: 7, of which 6 were waited for; matrix products, arithmetic and copies ran while one was open for 3% of the time, Pallas kernels for 0%

commit v1 on v0

v1 whole, which is shorter than its diff:
```python
import functools

import jax
import jax.numpy as jnp
from jax import lax
from jax.experimental import pallas as pl
from jax.experimental.pallas import tpu as pltpu
from jax.sharding import PartitionSpec as P

TILE = 256
HALF = 128
LEAF = 64
MESH = pl.DeviceIdType.MESH
HIGHEST = lax.Precision.HIGHEST
F32 = jnp.float32
BF16 = jnp.bfloat16


def dot(left, right, contract, precision=None):
    return lax.dot_general(
        left, right, (contract, ((), ())), precision=precision, preferred_element_type=F32
    )


def split3(value):
    high = value.astype(BF16)
    rest = value - high.astype(F32)
    mid = rest.astype(BF16)
    low = (rest - mid.astype(F32)).astype(BF16)
    return high, mid, low


def split2(value):
    high = value.astype(BF16)
    return high, (value - high.astype(F32)).astype(BF16)


def permuted(tile, row_of, col_of):
    height, width = row_of.shape[0], col_of.shape[0]
    high, mid, low = split3(tile)
    nt = ((1,), (1,))
    moved = dot(high, col_of, nt) + dot(mid, col_of, nt) + dot(low, col_of, nt)
    high, mid, low = split3(moved)
    nn = ((1,), (0,))
    return dot(row_of, high, nn) + dot(row_of, mid, nn) + dot(row_of, low, nn)


def one_hot(places, count):
    rows = lax.broadcasted_iota(jnp.int32, (count, places.shape[1]), 0)
    return jnp.where(rows == places, 1.0, 0.0).astype(BF16)


def leaf_inverse(block):
    n = block.shape[0]
    rows = lax.broadcasted_iota(jnp.int32, (n, n), 0)
    lanes = lax.broadcasted_iota(jnp.int32, (n, n), 1)
    row_ids = lax.broadcasted_iota(jnp.int32, (n, 1), 0)
    work = block
    for j in range(n - 1):
        column = work[:, j : j + 1]
        row = work[j : j + 1, :]
        pivot = work[j : j + 1, j : j + 1]
        factor = jnp.where(row_ids > j, column * (1.0 / pivot), 0.0)
        changed = work - factor * row
        work = jnp.where(lanes == j, jnp.where(rows > j, -factor, work), changed)
    pivots = jnp.sum(jnp.where(rows == lanes, work, 0.0), axis=1, keepdims=True)
    unit = jnp.where(lanes < rows, work, jnp.where(lanes == rows, 1.0, 0.0))
    return unit * lax.rsqrt(pivots)


def exchange_kernel(
    front_ref, tile_ref, child_ref, row_places_ref, col_places_ref,
    left_ref, right_ref, inverse_ref, child_out_ref,
    made, early, corner, work, strip, send_sems, left_sems, right_sems, inverse_sems,
    child_sems, corner_sems, local_sems,
):
    s = lax.axis_index("sub")
    r = lax.axis_index("row")
    c = lax.axis_index("col")
    z, h, k = c // 4, (c // 2) % 2, c % 2
    g = 4 * s + r

    def col_of(zz, hh, kk):
        return zz * 4 + hh * 2 + kk

    def at(ss=None, rr=None, cc=None):
        return (s if ss is None else ss, c if cc is None else cc, r if rr is None else rr)

    z_up, z_down = (z + 1) % 8, (z + 7) % 8
    to_up = at(cc=col_of(z_up, h, k))
    to_down = at(cc=col_of(z_down, h, k))
    to_far = at(cc=col_of(z, 1 - h, k))
    to_twin = at(cc=col_of(z, h, 1 - k))
    to_sub = at(ss=1 - s)

    def to_row(rr):
        return at(rr=rr)

    barrier = pltpu.get_barrier_semaphore()
    friends = [to_up, to_down, to_far, to_twin, to_sub]
    for step in (1, 2, 3):
        friends.append(at(rr=(r + step) % 4))
        friends.append(at(ss=1 - s, rr=(r + step) % 4))
    for friend in friends:
        pl.semaphore_signal(barrier, inc=1, device_id=friend, device_id_type=MESH)
    pl.semaphore_wait(barrier, len(friends))

    pending = []
    used = [0]

    def slot():
        used[0] += 1
        return send_sems.at[used[0] - 1]

    def send(conditions, source, target, arrive, device):
        copy = pltpu.make_async_remote_copy(
            src_ref=source, dst_ref=target, send_sem=slot(), recv_sem=arrive,
            device_id=device, device_id_type=MESH,
        )
        condition = functools.reduce(jnp.logical_and, conditions)

        @pl.when(condition)
        def _():
            copy.start()

        pending.append((condition, copy))

    def await_at(target, arrive):
        pltpu.make_async_remote_copy(
            src_ref=target, dst_ref=target, send_sem=send_sems.at[0], recv_sem=arrive,
            device_id=to_twin, device_id_type=MESH,
        ).wait_recv()

    always = jnp.bool_(True)
    first = s == 0
    maker = jnp.logical_and(s == 0, r < 2)
    sender_early = jnp.logical_and(s == 1, r < 2)

    send(
        [sender_early],
        child_ref.at[0, pl.ds(0, TILE), :], early, child_sems.at[4], to_sub,
    )

    def send_children(condition):
        for m in range(4):
            place = pl.multiple_of((2 * m + 1 - s) * TILE, TILE)
            send(
                [condition],
                child_ref.at[0, pl.ds(place, TILE), :], child_out_ref.at[m],
                child_sems.at[m], to_sub,
            )

    send_children(jnp.logical_not(maker))

    @pl.when(maker)
    def _():
        await_at(early, child_sems.at[4])
        total = front_ref[...]
        for source in range(2):
            tile = tile_ref[0] if source == 0 else early[...]
            total = total + permuted(
                tile,
                one_hot(row_places_ref[source : source + 1, :], TILE),
                one_hot(col_places_ref[source : source + 1, :], 2 * TILE),
            )
        made[...] = total.reshape(2, HALF, 2 * TILE)

    own_left = c % 8 == g
    left_block = c // 8
    left_group = c % 8
    goal = at(ss=left_group // 4, rr=left_group % 4)
    local_copies = []

    def copy_here(conditions, source, target, number):
        copy = pltpu.make_async_copy(source, target, local_sems.at[number])
        condition = functools.reduce(jnp.logical_and, conditions)

        @pl.when(condition)
        def _():
            copy.start()

        local_copies.append((condition, copy))

    for part in range(2):
        send(
            [first, r == 0, c == 0],
            made.at[part, :, pl.ds(0, TILE)], corner.at[part], corner_sems.at[part],
            at(cc=1),
        )
    for panel in range(2):
        for part in range(2):
            q = 2 * panel + part
            send(
                [first, r == panel, jnp.logical_not(own_left)],
                made.at[part], left_ref.at[left_block, q],
                left_sems.at[left_block, q], goal,
            )
            copy_here(
                [first, r == panel, own_left],
                made.at[part], left_ref.at[left_block, q], q,
            )
            copy_here([first, r == panel], made.at[part], right_ref.at[q], 4 + q)
    for panel in range(2):
        for part in range(2):
            q = 2 * panel + part
            here = [first, r == panel]
            for target in (to_sub, to_row((panel + 1) % 4), to_row((panel + 3) % 4)):
                send(here, made.at[part], right_ref.at[q], right_sems.at[q], target)
    send_children(maker)
    for condition, copy in local_copies:
        pl.when(condition)(copy.wait)

    rides = k == r % 2
    home = h == r // 2
    even = z % 2 == s
    source_rider = jnp.logical_and(rides, even)
    other_rider = jnp.logical_and(rides, jnp.logical_not(even))
    mine = (z // 2) % 4

    def await_left(conditions, m, q):
        condition = functools.reduce(jnp.logical_and, conditions)

        @pl.when(condition)
        def _():
            await_at(left_ref.at[m, q], left_sems.at[m, q])

    def pass_left(conditions, m, q, devices):
        for device in devices:
            send(conditions, left_ref.at[m, q], left_ref.at[m, q], left_sems.at[m, q], device)

    not_made = [
        jnp.logical_not(jnp.logical_and(home, jnp.logical_and(first, r == panel)))
        for panel in range(2)
    ]
    home_source = jnp.logical_and(source_rider, home)
    far_source = jnp.logical_and(source_rider, jnp.logical_not(home))
    for q in range(4):
        await_left([home_source, not_made[q // 2]], mine, q)
        pass_left([home_source], mine, q, [to_far, to_up, to_down, to_twin])

    for panel in range(2):
        near, far, last = (panel + 1) % 4, (panel + 3) % 4, (panel + 2) % 4
        passer = far if panel == 0 else near
        for part in range(2):
            q = 2 * panel + part

            @pl.when(jnp.logical_not(jnp.logical_and(first, r == panel)))
            def _():
                await_at(right_ref.at[q], right_sems.at[q])

            send(
                [jnp.logical_not(first), r == panel],
                right_ref.at[q], right_ref.at[q], right_sems.at[q], to_row(near),
            )
            send(
                [jnp.logical_not(first), r == panel],
                right_ref.at[q], right_ref.at[q], right_sems.at[q], to_row(far),
            )
            send(
                [r == passer],
                right_ref.at[q], right_ref.at[q], right_sems.at[q], to_row(last),
            )

    chief = jnp.logical_and(jnp.logical_and(first, r == 0), c == 1)
    blocks = 2 * TILE // LEAF

    @pl.when(chief)
    def _():
        for part in range(2):
            await_at(corner.at[part], corner_sems.at[part])
        for q in range(4):
            pltpu.make_async_copy(
                right_ref.at[q, :, pl.ds(0, TILE)], strip.at[q], local_sems.at[8 + q]
            ).start()
        for q in range(4):
            pltpu.make_async_copy(
                right_ref.at[q, :, pl.ds(0, TILE)], strip.at[q], local_sems.at[8 + q]
            ).wait()
        work[0:TILE, 0:TILE] = corner[...].reshape(TILE, TILE)
        work[0:TILE, TILE:] = strip[0:2].reshape(TILE, TILE)
        work[TILE:, TILE:] = strip[2:4].reshape(TILE, TILE)
        work[TILE:, 0:TILE] = jnp.zeros((TILE, TILE), F32)

    lanes = lax.broadcasted_iota(jnp.int32, (1, 2 * TILE), 1)
    w_children = [
        ([k == 1], to_twin),
        ([k == 1, z <= 3], to_up),
        ([k == 1, jnp.logical_or(z == 0, z > 5)], to_down),
        ([k == 1, z == 0, h == 0], to_far),
        ([k == 1, z == 0, h == 0, first], to_sub),
        ([k == 1, z == 0, h == 0, first, r == 0], to_row(1)),
        ([k == 1, z == 0, h == 0, first, r == 0], to_row(3)),
        ([k == 1, z == 0, h == 0, first, r == 1], to_row(2)),
    ]

    def send_inverse(b, conditions):
        for more, device in w_children:
            send(
                conditions + more,
                inverse_ref.at[b], inverse_ref.at[b], inverse_sems.at[b], device,
            )

    for b in range(blocks):
        low, high = b * LEAF, (b + 1) * LEAF

        @pl.when(chief)
        def _():
            rows = work[low:high, :]
            leaf = leaf_inverse(rows[:, low:high])
            placed = jnp.concatenate(
                ([jnp.zeros((LEAF, low), F32)] if low else [])
                + [jnp.where(
                    lax.broadcasted_iota(jnp.int32, (LEAF, LEAF), 0)
                    == lax.broadcasted_iota(jnp.int32, (LEAF, LEAF), 1), 1.0, 0.0)]
                + ([jnp.zeros((LEAF, 2 * TILE - high), F32)] if high < 2 * TILE else []),
                axis=1,
            )
            in_block = jnp.logical_and(lanes >= low, lanes < high)
            rows = jnp.where(in_block, placed, rows)
            product = dot(leaf, rows, ((1,), (0,)), HIGHEST)
            made_inverse = jnp.where(lanes < high, product, 0.0)
            early_rows = made_inverse
            work[low:high, :] = early_rows
            if high < 2 * TILE:
                later = product[:, high:]
                below = jnp.where(in_block, 0.0, work[high:, :])
                work[high:, :] = below - dot(later, product, ((0,), (0,)), HIGHEST)
            copy = pltpu.make_async_copy(
                work.at[pl.ds(low, LEAF), :], inverse_ref.at[b], local_sems.at[12]
            )
            copy.start()
            copy.wait()

        send_inverse(b, [chief])

    for q in range(4):
        await_left([far_source], mine, q)
        pass_left([far_source], mine, q, [to_up, to_down, to_twin])
    above, below = (mine + 1) % 4, (mine + 3) % 4
    across = (mine + 2) % 4
    block_down = ((z + 7 - s) // 2) % 4
    block_up = ((z + 1 + 8 - s) // 2) % 4
    for q in range(4):
        await_left([other_rider], block_down, q)
        pass_left([other_rider], block_down, q, [to_up, to_twin])
        await_left([other_rider], block_up, q)
        pass_left([other_rider], block_up, q, [to_down, to_twin])
        await_left([source_rider], below, q)
        pass_left([source_rider], below, q, [to_up, to_twin])
        await_left([source_rider], above, q)
        pass_left([source_rider], above, q, [to_down, to_twin])
    far_down, far_up = (block_down + 3) % 4, (block_up + 1) % 4
    for q in range(4):
        await_left([other_rider], far_down, q)
        pass_left([other_rider], far_down, q, ([to_up] if q < 2 else []) + [to_twin])
        await_left([other_rider], far_up, q)
        pass_left([other_rider], far_up, q, ([to_down] if q >= 2 else []) + [to_twin])
        await_left([source_rider], across, q)
        pass_left([source_rider], across, q, [to_twin])

    for b in range(blocks):
        @pl.when(jnp.logical_not(chief))
        def _():
            await_at(inverse_ref.at[b], inverse_sems.at[b])

        send_inverse(b, [jnp.logical_not(chief)])

    for m in range(4):
        for q in range(4):
            await_left([jnp.logical_not(rides)], m, q)
    for m in range(4):
        await_at(child_out_ref.at[m], child_sems.at[m])
    for condition, copy in pending:
        pl.when(condition)(copy.wait_send)


SENDS = 320


def exchange(front_in, child_update, row_places, col_places):
    blocks = 2 * TILE // LEAF
    outs = (
        jax.ShapeDtypeStruct((4, 4, HALF, 2 * TILE), F32),
        jax.ShapeDtypeStruct((4, HALF, 2 * TILE), F32),
        jax.ShapeDtypeStruct((blocks, LEAF, 2 * TILE), F32),
        jax.ShapeDtypeStruct((4, TILE, TILE), F32),
    )
    return pl.pallas_call(
        exchange_kernel,
        out_shape=outs,
        grid=(1,),
        in_specs=[
            pl.BlockSpec((TILE, 2 * TILE), lambda i: (0, 0)),
            pl.BlockSpec((1, TILE, TILE), lambda i: (0, 0, 0)),
            pl.BlockSpec(memory_space=pl.ANY),
            pl.BlockSpec((2, TILE), lambda i: (0, 0)),
            pl.BlockSpec((2, TILE), lambda i: (0, 0)),
        ],
        out_specs=[pl.BlockSpec(memory_space=pl.ANY)] * 4,
        scratch_shapes=[
            pltpu.VMEM((2, HALF, 2 * TILE), F32),
            pltpu.VMEM((TILE, TILE), F32),
            pltpu.VMEM((2, HALF, TILE), F32),
            pltpu.VMEM((2 * TILE, 2 * TILE), F32),
            pltpu.VMEM((4, HALF, TILE), F32),
            pltpu.SemaphoreType.DMA((SENDS,)),
            pltpu.SemaphoreType.DMA((4, 4)),
            pltpu.SemaphoreType.DMA((4,)),
            pltpu.SemaphoreType.DMA((blocks,)),
            pltpu.SemaphoreType.DMA((5,)),
            pltpu.SemaphoreType.DMA((2,)),
            pltpu.SemaphoreType.DMA((13,)),
        ],
        compiler_params=pltpu.CompilerParams(
            collective_id=0, has_side_effects=True, vmem_limit_bytes=48 * 1024 * 1024
        ),
        name="exchange",
    )(front_in, child_update, child_update, row_places, col_places)


def update_kernel(
    facts_ref, front_ref, mine_ref, other_ref, row_places_ref, col_places_ref,
    left_ref, right_ref, inverse_ref, out_ref, right_high, right_low,
):
    i = pl.program_id(0)
    s, r, c = facts_ref[0], facts_ref[1], facts_ref[2]
    g = 4 * s + r
    number = g + 8 * i
    inverse = inverse_ref[...].reshape(2 * TILE, 2 * TILE)

    @pl.when(i == 0)
    def _():
        done = dot(inverse, right_ref[...].reshape(2 * TILE, 2 * TILE), ((1,), (0,)), HIGHEST)
        high, low = split2(done)
        right_high[...] = high
        right_low[...] = low

    left = left_ref[...].reshape(2 * TILE, TILE)
    done = dot(left, inverse, ((0,), (1,)), HIGHEST)
    high, low = split2(done)
    nn = ((1,), (0,))
    update = (
        dot(high, right_high[...], nn) + dot(high, right_low[...], nn)
        + dot(low, right_high[...], nn)
    )
    out_ref[...] = front_ref[...] - update
    for source in range(2):
        lands = facts_ref[4 + 4 * source + i % 4] == i // 4

        @pl.when(lands)
        def _():
            tile = jnp.where(s == source, mine_ref[0], other_ref[0])
            moved = permuted(
                tile,
                one_hot(row_places_ref[0, source : source + 1, :], TILE),
                one_hot(col_places_ref[source : source + 1, :], TILE),
            )
            place = pl.multiple_of(facts_ref[12 + source] * TILE, TILE)
            out_ref[:, pl.ds(place, TILE)] += moved

    @pl.when(jnp.logical_and(c < 2, number >= 0))
    def _():
        panel = jnp.where(c == 0, done[:, :TILE], done[:, TILE:])
        rows = lax.broadcasted_iota(jnp.int32, (TILE, TILE), 0)
        lanes = lax.broadcasted_iota(jnp.int32, (TILE, TILE), 1)
        keep = jnp.logical_or(number > c, jnp.logical_and(number == c, lanes <= rows))
        out_ref[:, 0:TILE] = jnp.where(keep, panel, 0.0)

    @pl.when(number < 2)
    def _():
        out_ref[:, TILE:] = jnp.zeros((TILE, TILE), F32)

    @pl.when(jnp.logical_and(number < 2, c >= 2))
    def _():
        out_ref[:, 0:TILE] = jnp.zeros((TILE, TILE), F32)


def update(facts, front_in, child_update, arrived, row_places, col_places, left, right, inverse):
    blocks = 2 * TILE // LEAF
    grid_spec = pltpu.PrefetchScalarGridSpec(
        num_scalar_prefetch=1,
        grid=(8,),
        in_specs=[
            pl.BlockSpec((TILE, 2 * TILE), lambda i, f: (i, 0)),
            pl.BlockSpec((1, TILE, TILE), lambda i, f: (0, f[0] + 2 * (i % 4), 0)),
            pl.BlockSpec((1, TILE, TILE), lambda i, f: (i % 4, 0, 0)),
            pl.BlockSpec((1, 2, TILE), lambda i, f: (i % 4, 0, 0)),
            pl.BlockSpec((2, TILE), lambda i, f: (0, 0)),
            pl.BlockSpec((1, 4, HALF, TILE), lambda i, f: (i % 4, 0, 0, i // 4)),
            pl.BlockSpec((4, HALF, 2 * TILE), lambda i, f: (0, 0, 0)),
            pl.BlockSpec((blocks, LEAF, 2 * TILE), lambda i, f: (0, 0, 0)),
        ],
        out_specs=pl.BlockSpec((TILE, 2 * TILE), lambda i, f: (i, 0)),
        scratch_shapes=[
            pltpu.VMEM((2 * TILE, 2 * TILE), BF16),
            pltpu.VMEM((2 * TILE, 2 * TILE), BF16),
        ],
    )
    return pl.pallas_call(
        update_kernel,
        out_shape=jax.ShapeDtypeStruct((8 * TILE, 2 * TILE), F32),
        grid_spec=grid_spec,
        compiler_params=pltpu.CompilerParams(vmem_limit_bytes=48 * 1024 * 1024),
        name="update",
    )(facts, front_in, child_update, arrived, row_places, col_places, left, right, inverse)


def local(front_in, child_update, child_map):
    s = lax.axis_index("sub")
    r = lax.axis_index("row")
    c = lax.axis_index("col")
    g = 4 * s + r
    tiles = child_map.reshape(2, 32, TILE)
    col_map = lax.dynamic_index_in_dim(tiles, c, 1, keepdims=False)
    row_map = lax.dynamic_index_in_dim(tiles.reshape(2, 4, 8, TILE), g, 2, keepdims=False)
    early_rows = row_map[:, 0] - g * TILE
    early_cols = col_map // (32 * TILE) * TILE + col_map % TILE
    left, right, inverse, arrived = exchange(front_in, child_update, early_rows, early_cols)
    facts = jnp.concatenate(
        [
            jnp.stack([s, r, c, 0 * s]).astype(jnp.int32),
            (row_map[:, :, 0] // (32 * TILE)).reshape(-1),
            col_map[:, 0] // (32 * TILE),
        ]
    )
    return update(
        facts, front_in, child_update, arrived,
        jnp.swapaxes(row_map % TILE, 0, 1), col_map % TILE, left, right, inverse,
    )


def solution(mesh):
    placed = (P(("sub", "row"), "col"), P("sub", "row", "col"), P())
    return jax.shard_map(
        local, mesh=mesh, in_specs=placed, out_specs=P(("sub", "row"), "col"), check_vma=False
    )
```

time: 1160 us -> 138 us (0.12)
  the two profiles are of different devices: /device:TPU:60 before, /device:TPU:158 now
where the time goes in v1:
time: 138 us
  Pallas kernels  134 us (97%)
  local copies, waits for them, and re-layouts  2.84 us (2%)
    pallas_call x1, Pallas kernels, exchange(): pl.pallas_call(exchange_kernel, out_shape=outs, grid=(1,), in_specs=[pl.B...  111 us
    pallas_call x1, Pallas kernels, update(): pl.pallas_call(update_kernel, out_shape=jax.ShapeDtypeStruct((8 * TILE, 2...  23.5 us

profile of v1, /device:TPU:158, one launch (start us, length us, event | category | flops | bytes accessed | tf_op | source)
XLA Modules:
  0.0 137.7 jit_solution(13969125425197899973)
XLA Ops:
  0.0 0.7 multiply_add_fusion
  0.7 0.1 slice_reduce_fusion
  0.8 0.8 copy.16
  1.7 0.1 copy.8
  1.8 0.1 squeeze.16
  1.9 0.1 concatenate.3.facts_ref
  2.0 0.0 copy-start
  2.0 1.6 %copy-done = f32[1,2048,256]{2,1,0:T(8,128)S(1)} copy-done((f32[1,2048,256]{2,1,0:T(8,128)S(1)}, f32[1,2048,256]{2,1,0:T(8,128)}, u32[]{:S(2)}) %copy-start) | copy-done | bytes 2097176
  3.6 110.5 %exchange.1 = (f32[4,4,128,512]{3,2,1,0:T(8,128)}, f32[4,128,512]{2,1,0:T(8,128)S(1)}, f32[8,64,512]{2,1,0:T(8,128)S(1)}, f32[4,256,256]{2,1,0:T(8,128)S(1)}) custom-call(f32[2048,512]{1,0:T(8,128)} %front_ref.3, f32[1,2048,256]{2,1,0:T(8,128)S(1)} %copy-done, f32[1,2048,256]{2,1,0:T(8,128)S(1)} %copy-done, s32[2,256]{1,0:T(2,128)S(1)} %fusion.2.row_places_ref, ...), custom_call_target="tpu_custom_call" | custom-call | tf_op jit(solution)/shard_map/exchange/pallas_call | solution.py:388
  114.1 23.5 %update.1 = f32[2048,512]{1,0:T(8,128)} custom-call(s32[14]{0:T(128)S(1)} %concatenate.3.facts_ref, f32[2048,512]{1,0:T(8,128)} %front_ref.3, f32[1,2048,256]{2,1,0:T(8,128)S(1)} %copy-done, f32[4,256,256]{2,1,0:T(8,128)S(1)} %get-tuple-element.9.other_ref, s32[4,2,256]{2,1,0:T(2,128)S(1)} %fusion.row_places_ref, ...), custom_call_target="tpu_custom_call" | custom-call | tf_op jit(solution)/shard_map/update/pallas_call | solution.py:499
  (7 shorter events, 0.1 us)
Async XLA Ops:
  2.0 1.6 %copy-start = (f32[1,2048,256]{2,1,0:T(8,128)S(1)}, f32[1,2048,256]{2,1,0:T(8,128)}, u32[]{:S(2)}) copy-start(f32[1,2048,256]{2,1,0:T(8,128)} %mine_ref.1) | copy-start | bytes 6291460

commit v2 on v1

--- a/solution.py
+++ b/solution.py
@@ -10,6 +10,8 @@
 TILE = 256
 HALF = 128
 LEAF = 64
+PARTS = 4
+RUN = 2 * TILE // PARTS
 MESH = pl.DeviceIdType.MESH
 HIGHEST = lax.Precision.HIGHEST
 F32 = jnp.float32
@@ -33,6 +35,13 @@
 def split2(value):
     high = value.astype(BF16)
     return high, (value - high.astype(F32)).astype(BF16)
+
+
+def dot3(left, right, contract):
+    return (
+        dot(left[0], right[0], contract) + dot(left[0], right[1], contract)
+        + dot(left[1], right[0], contract)
+    )
 
 
 def permuted(tile, row_of, col_of):
@@ -52,26 +61,51 @@
 
 def leaf_inverse(block):
     n = block.shape[0]
+    count = n // 8
+    rows = lax.broadcasted_iota(jnp.int32, (8, n), 0)
+    lanes = lax.broadcasted_iota(jnp.int32, (8, n), 1)
+    slabs = [block[8 * t : 8 * t + 8, :] for t in range(count)]
+    for t in range(count):
+        base = 8 * t
+        spread = [
+            [jnp.broadcast_to(slabs[u][:, base + k : base + k + 1], (8, n)) for u in range(t, count)]
+            for k in range(8)
+        ]
+        pivots = None
+        for j in range(8):
+            pivot = spread[j][0][j : j + 1, :]
+            inverse = reciprocal(pivot)
+            heads = [spread[k][0][j : j + 1, :] * inverse for k in range(j + 1, 8)]
+            scaled = slabs[t][j : j + 1, :] * inverse
+            everywhere = jnp.broadcast_to(pivot, (8, n))
+            pivots = everywhere if j == 0 else jnp.where(rows == j, everywhere, pivots)
+            for u in range(t, count):
+                factor = spread[j][u - t]
+                if u == t:
+                    factor = jnp.where(rows > j, factor, 0.0)
+                for k in range(j + 1, 8):
+                    spread[k][u - t] = spread[k][u - t] - factor * heads[k - j - 1]
+                changed = slabs[u] - factor * scaled
+                entry = -(factor * inverse)
+                if u == t:
+                    entry = jnp.where(rows > j, entry, jnp.where(rows == j, 1.0, slabs[u]))
+                slabs[u] = jnp.where(lanes == base + j, entry, changed)
+        slabs[t] = slabs[t] * lax.rsqrt(pivots)
+    whole = jnp.concatenate(slabs, axis=0)
     rows = lax.broadcasted_iota(jnp.int32, (n, n), 0)
     lanes = lax.broadcasted_iota(jnp.int32, (n, n), 1)
-    row_ids = lax.broadcasted_iota(jnp.int32, (n, 1), 0)
-    work = block
-    for j in range(n - 1):
-        column = work[:, j : j + 1]
-        row = work[j : j + 1, :]
-        pivot = work[j : j + 1, j : j + 1]
-        factor = jnp.where(row_ids > j, column * (1.0 / pivot), 0.0)
-        changed = work - factor * row
-        work = jnp.where(lanes == j, jnp.where(rows > j, -factor, work), changed)
-    pivots = jnp.sum(jnp.where(rows == lanes, work, 0.0), axis=1, keepdims=True)
-    unit = jnp.where(lanes < rows, work, jnp.where(lanes == rows, 1.0, 0.0))
-    return unit * lax.rsqrt(pivots)
+    return jnp.where(lanes <= rows, whole, 0.0)
+
+
+def reciprocal(value):
+    guess = pltpu.reciprocal(value, approx=True)
+    return guess * (2.0 - value * guess)
 
 
 def exchange_kernel(
     front_ref, tile_ref, child_ref, row_places_ref, col_places_ref,
     left_ref, right_ref, inverse_ref, child_out_ref,
-    made, early, corner, work, strip, send_sems, left_sems, right_sems, inverse_sems,
+    made, turned, early, corner, work, strip, send_sems, left_sems, right_sems, inverse_sems,
     child_sems, corner_sems, local_sems,
 ):
     s = lax.axis_index("sub")
@@ -101,6 +135,9 @@
     for step in (1, 2, 3):
         friends.append(at(rr=(r + step) % 4))
         friends.append(at(ss=1 - s, rr=(r + step) % 4))
+        friends.append(at(rr=(r + step) % 4, cc=col_of(z, 1 - h, k)))
+        friends.append(at(ss=1 - s, rr=(r + step) % 4, cc=col_of(z, 1 - h, k)))
+    friends.append(at(ss=1 - s, cc=col_of(z, 1 - h, k)))
     for friend in friends:
         pl.semaphore_signal(barrier, inc=1, device_id=friend, device_id_type=MESH)
     pl.semaphore_wait(barrier, len(friends))
@@ -141,16 +178,16 @@
         child_ref.at[0, pl.ds(0, TILE), :], early, child_sems.at[4], to_sub,
     )
 
-    def send_children(condition):
-        for m in range(4):
+    def send_children(numbers):
+        for m in numbers:
             place = pl.multiple_of((2 * m + 1 - s) * TILE, TILE)
             send(
-                [condition],
+                [always],
                 child_ref.at[0, pl.ds(place, TILE), :], child_out_ref.at[m],
                 child_sems.at[m], to_sub,
             )
 
-    send_children(jnp.logical_not(maker))
+    send_children((0, 1))
 
     @pl.when(maker)
     def _():
@@ -164,11 +201,13 @@
                 one_hot(col_places_ref[source : source + 1, :], 2 * TILE),
             )
         made[...] = total.reshape(2, HALF, 2 * TILE)
+        turned[...] = total.T
 
     own_left = c % 8 == g
     left_block = c // 8
     left_group = c % 8
     goal = at(ss=left_group // 4, rr=left_group % 4)
+    far_goal = at(ss=left_group // 4, rr=left_group % 4, cc=col_of(z, 1 - h, k))
     local_copies = []
 
     def copy_here(conditions, source, target, number):
@@ -187,26 +226,27 @@
             made.at[part, :, pl.ds(0, TILE)], corner.at[part], corner_sems.at[part],
             at(cc=1),
         )
+    def left_at(m, q):
+        return left_ref.at[m, q // PARTS, pl.ds(q % PARTS * RUN, RUN), :]
+
     for panel in range(2):
-        for part in range(2):
-            q = 2 * panel + part
+        here = [first, r == panel]
+        for part in range(PARTS):
+            q = PARTS * panel + part
+            piece = turned.at[pl.ds(part * RUN, RUN), :]
             send(
-                [first, r == panel, jnp.logical_not(own_left)],
-                made.at[part], left_ref.at[left_block, q],
-                left_sems.at[left_block, q], goal,
+                here + [jnp.logical_not(own_left)],
+                piece, left_at(left_block, q), left_sems.at[left_block, q], goal,
             )
-            copy_here(
-                [first, r == panel, own_left],
-                made.at[part], left_ref.at[left_block, q], q,
-            )
-            copy_here([first, r == panel], made.at[part], right_ref.at[q], 4 + q)
+            send(here, piece, left_at(left_block, q), left_sems.at[left_block, q], far_goal)
+        copy_here(here + [own_left], turned, left_ref.at[left_block, panel], panel)
+        copy_here(here, made, right_ref.at[pl.ds(2 * panel, 2)], 4 + panel)
     for panel in range(2):
         for part in range(2):
             q = 2 * panel + part
             here = [first, r == panel]
             for target in (to_sub, to_row((panel + 1) % 4), to_row((panel + 3) % 4)):
                 send(here, made.at[part], right_ref.at[q], right_sems.at[q], target)
-    send_children(maker)
     for condition, copy in local_copies:
         pl.when(condition)(copy.wait)
 
@@ -222,44 +262,51 @@
 
         @pl.when(condition)
         def _():
-            await_at(left_ref.at[m, q], left_sems.at[m, q])
+            await_at(left_at(m, q), left_sems.at[m, q])
 
     def pass_left(conditions, m, q, devices):
         for device in devices:
-            send(conditions, left_ref.at[m, q], left_ref.at[m, q], left_sems.at[m, q], device)
+            send(conditions, left_at(m, q), left_at(m, q), left_sems.at[m, q], device)
 
     not_made = [
         jnp.logical_not(jnp.logical_and(home, jnp.logical_and(first, r == panel)))
         for panel in range(2)
     ]
-    home_source = jnp.logical_and(source_rider, home)
-    far_source = jnp.logical_and(source_rider, jnp.logical_not(home))
-    for q in range(4):
-        await_left([home_source, not_made[q // 2]], mine, q)
-        pass_left([home_source], mine, q, [to_far, to_up, to_down, to_twin])
-
-    for panel in range(2):
-        near, far, last = (panel + 1) % 4, (panel + 3) % 4, (panel + 2) % 4
-        passer = far if panel == 0 else near
-        for part in range(2):
-            q = 2 * panel + part
-
-            @pl.when(jnp.logical_not(jnp.logical_and(first, r == panel)))
-            def _():
-                await_at(right_ref.at[q], right_sems.at[q])
-
-            send(
-                [jnp.logical_not(first), r == panel],
-                right_ref.at[q], right_ref.at[q], right_sems.at[q], to_row(near),
-            )
-            send(
-                [jnp.logical_not(first), r == panel],
-                right_ref.at[q], right_ref.at[q], right_sems.at[q], to_row(far),
-            )
-            send(
-                [r == passer],
-                right_ref.at[q], right_ref.at[q], right_sems.at[q], to_row(last),
-            )
+    for q in range(2 * PARTS):
+        await_left([source_rider, not_made[q // PARTS]], mine, q)
+        pass_left([source_rider], mine, q, [to_up, to_down, to_twin])
+
+    def pass_right(who):
+        for panel in range(2):
+            near, far, last = (panel + 1) % 4, (panel + 3) % 4, (panel + 2) % 4
+            passer = far if panel == 0 else near
+            for part in range(2):
+                q = 2 * panel + part
+                turn = jnp.logical_and(jnp.logical_not(first), r == panel)
+                passes = jnp.logical_and(who, jnp.logical_or(turn, r == passer))
+
+                @pl.when(passes)
+                def _():
+                    await_at(right_ref.at[q], right_sems.at[q])
+
+                for condition, target in ((turn, near), (turn, far), (r == passer, last)):
+                    send(
+                        [who, condition],
+                        right_ref.at[q], right_ref.at[q], right_sems.at[q], to_row(target),
+                    )
+
+    def await_right(who):
+        for panel in range(2):
+            passer = (panel + 3) % 4 if panel == 0 else (panel + 1) % 4
+            for part in range(2):
+                q = 2 * panel + part
+                done = jnp.logical_or(r == panel, r == passer)
+
+                @pl.when(jnp.logical_and(who, jnp.logical_not(done)))
+                def _():
+                    await_at(right_ref.at[q], right_sems.at[q])
+
+    pass_right(jnp.logical_not(rides))
 
     chief = jnp.logical_and(jnp.logical_and(first, r == 0), c == 1)
     blocks = 2 * TILE // LEAF
@@ -268,6 +315,7 @@
     def _():
         for part in range(2):
             await_at(corner.at[part], corner_sems.at[part])
+            await_at(right_ref.at[2 + part], right_sems.at[2 + part])
         for q in range(4):
             pltpu.make_async_copy(
                 right_ref.at[q, :, pl.ds(0, TILE)], strip.at[q], local_sems.at[8 + q]
@@ -284,20 +332,24 @@
     lanes = lax.broadcasted_iota(jnp.int32, (1, 2 * TILE), 1)
     w_children = [
         ([k == 1], to_twin),
-        ([k == 1, z <= 3], to_up),
-        ([k == 1, jnp.logical_or(z == 0, z > 5)], to_down),
-        ([k == 1, z == 0, h == 0], to_far),
-        ([k == 1, z == 0, h == 0, first], to_sub),
-        ([k == 1, z == 0, h == 0, first, r == 0], to_row(1)),
-        ([k == 1, z == 0, h == 0, first, r == 0], to_row(3)),
-        ([k == 1, z == 0, h == 0, first, r == 1], to_row(2)),
-    ]
+        ([k == 1, r == 0], to_row(1)),
+        ([k == 1, r == 0], to_row(3)),
+        ([k == 1, r == 1], to_row(2)),
+        ([k == 1, r == 0, first], to_sub),
+        ([k == 1, r == 0, first, h == 0], to_far),
+        ([k == 1, r == 0, first, h == 0, z <= 3], to_up),
+        ([k == 1, r == 0, first, h == 0, jnp.logical_or(z == 0, z > 5)], to_down),
+    ][::-1]
+
+    def inverse_at(b):
+        reach = ((b + 1) * LEAF + HALF - 1) // HALF * HALF
+        return inverse_ref.at[b, :, pl.ds(0, reach)]
 
     def send_inverse(b, conditions):
         for more, device in w_children:
             send(
                 conditions + more,
-                inverse_ref.at[b], inverse_ref.at[b], inverse_sems.at[b], device,
+                inverse_at(b), inverse_at(b), inverse_sems.at[b], device,
             )
 
     for b in range(blocks):
@@ -333,14 +385,11 @@
 
         send_inverse(b, [chief])
 
-    for q in range(4):
-        await_left([far_source], mine, q)
-        pass_left([far_source], mine, q, [to_up, to_down, to_twin])
     above, below = (mine + 1) % 4, (mine + 3) % 4
     across = (mine + 2) % 4
     block_down = ((z + 7 - s) // 2) % 4
     block_up = ((z + 1 + 8 - s) // 2) % 4
-    for q in range(4):
+    for q in range(2 * PARTS):
         await_left([other_rider], block_down, q)
         pass_left([other_rider], block_down, q, [to_up, to_twin])
         await_left([other_rider], block_up, q)
@@ -349,24 +398,27 @@
         pass_left([source_rider], below, q, [to_up, to_twin])
         await_left([source_rider], above, q)
         pass_left([source_rider], above, q, [to_down, to_twin])
+    pass_right(rides)
+    send_children((2, 3))
     far_down, far_up = (block_down + 3) % 4, (block_up + 1) % 4
-    for q in range(4):
+    for q in range(2 * PARTS):
         await_left([other_rider], far_down, q)
-        pass_left([other_rider], far_down, q, ([to_up] if q < 2 else []) + [to_twin])
+        pass_left([other_rider], far_down, q, ([to_up] if q < PARTS else []) + [to_twin])
         await_left([other_rider], far_up, q)
-        pass_left([other_rider], far_up, q, ([to_down] if q >= 2 else []) + [to_twin])
+        pass_left([other_rider], far_up, q, ([to_down] if q >= PARTS else []) + [to_twin])
         await_left([source_rider], across, q)
         pass_left([source_rider], across, q, [to_twin])
 
     for b in range(blocks):
         @pl.when(jnp.logical_not(chief))
         def _():
-            await_at(inverse_ref.at[b], inverse_sems.at[b])
+            await_at(inverse_at(b), inverse_sems.at[b])
 
         send_inverse(b, [jnp.logical_not(chief)])
 
+    await_right(jnp.logical_not(chief))
     for m in range(4):
-        for q in range(4):
+        for q in range(2 * PARTS):
             await_left([jnp.logical_not(rides)], m, q)
     for m in range(4):
         await_at(child_out_ref.at[m], child_sems.at[m])
@@ -374,13 +426,13 @@
         pl.when(condition)(copy.wait_send)
 
 
-SENDS = 320
+SENDS = 400
 
 
 def exchange(front_in, child_update, row_places, col_places):
     blocks = 2 * TILE // LEAF
     outs = (
-        jax.ShapeDtypeStruct((4, 4, HALF, 2 * TILE), F32),
+        jax.ShapeDtypeStruct((4, 2, 2 * TILE, TILE), F32),
         jax.ShapeDtypeStruct((4, HALF, 2 * TILE), F32),
         jax.ShapeDtypeStruct((blocks, LEAF, 2 * TILE), F32),
         jax.ShapeDtypeStruct((4, TILE, TILE), F32),
@@ -399,12 +451,13 @@
         out_specs=[pl.BlockSpec(memory_space=pl.ANY)] * 4,
         scratch_shapes=[
             pltpu.VMEM((2, HALF, 2 * TILE), F32),
+            pltpu.VMEM((2 * TILE, TILE), F32),
             pltpu.VMEM((TILE, TILE), F32),
             pltpu.VMEM((2, HALF, TILE), F32),
             pltpu.VMEM((2 * TILE, 2 * TILE), F32),
             pltpu.VMEM((4, HALF, TILE), F32),
             pltpu.SemaphoreType.DMA((SENDS,)),
-            pltpu.SemaphoreType.DMA((4, 4)),
+            pltpu.SemaphoreType.DMA((4, 2 * PARTS)),
             pltpu.SemaphoreType.DMA((4,)),
             pltpu.SemaphoreType.DMA((blocks,)),
             pltpu.SemaphoreType.DMA((5,)),
@@ -420,89 +473,102 @@
 
 def update_kernel(
     facts_ref, front_ref, mine_ref, other_ref, row_places_ref, col_places_ref,
-    left_ref, right_ref, inverse_ref, out_ref, right_high, right_low,
+    left_ref, right_ref, inverse_ref, out_ref, w_high, w_low, right_high, right_low,
 ):
-    i = pl.program_id(0)
+    m = pl.program_id(0)
     s, r, c = facts_ref[0], facts_ref[1], facts_ref[2]
     g = 4 * s + r
-    number = g + 8 * i
-    inverse = inverse_ref[...].reshape(2 * TILE, 2 * TILE)
-
-    @pl.when(i == 0)
+    nn, nt = ((1,), (0,)), ((1,), (1,))
+
+    def half_of(ref_high, ref_low, row, col):
+        rows, cols = pl.ds(row * TILE, TILE), pl.ds(col * TILE, TILE)
+        return ref_high[rows, cols], ref_low[rows, cols]
+
+    @pl.when(m == 0)
     def _():
-        done = dot(inverse, right_ref[...].reshape(2 * TILE, 2 * TILE), ((1,), (0,)), HIGHEST)
-        high, low = split2(done)
-        right_high[...] = high
-        right_low[...] = low
-
-    left = left_ref[...].reshape(2 * TILE, TILE)
-    done = dot(left, inverse, ((0,), (1,)), HIGHEST)
-    high, low = split2(done)
-    nn = ((1,), (0,))
-    update = (
-        dot(high, right_high[...], nn) + dot(high, right_low[...], nn)
-        + dot(low, right_high[...], nn)
-    )
-    out_ref[...] = front_ref[...] - update
+        rows = lax.broadcasted_iota(jnp.int32, (2 * TILE, 2 * TILE), 0)
+        lanes = lax.broadcasted_iota(jnp.int32, (2 * TILE, 2 * TILE), 1)
+        inverse = inverse_ref[...].reshape(2 * TILE, 2 * TILE)
+        w_high[...], w_low[...] = split2(jnp.where(lanes <= rows, inverse, 0.0))
+        high, low = split2(right_ref[...].reshape(2 * TILE, 2 * TILE))
+        upper = dot3(half_of(w_high, w_low, 0, 0), (high[:TILE], low[:TILE]), nn)
+        lower = dot3((w_high[TILE:], w_low[TILE:]), (high, low), nn)
+        right_high[:TILE], right_low[:TILE] = split2(upper)
+        right_high[TILE:], right_low[TILE:] = split2(lower)
+
+    first, second = split2(left_ref[0, 0]), split2(left_ref[0, 1])
+    done = (
+        dot3(first, half_of(w_high, w_low, 0, 0), nt),
+        dot3(first, half_of(w_high, w_low, 1, 0), nt)
+        + dot3(second, half_of(w_high, w_low, 1, 1), nt),
+    )
+    total = None
+    for part in range(2):
+        rows = pl.ds(part * TILE, TILE)
+        product = dot3(split2(done[part]), (right_high[rows, :], right_low[rows, :]), nn)
+        total = product if total is None else total + product
+    for half in range(2):
+        out_ref[half, 0] = front_ref[half, 0] - total[half * TILE : (half + 1) * TILE]
     for source in range(2):
-        lands = facts_ref[4 + 4 * source + i % 4] == i // 4
-
-        @pl.when(lands)
-        def _():
-            tile = jnp.where(s == source, mine_ref[0], other_ref[0])
-            moved = permuted(
-                tile,
-                one_hot(row_places_ref[0, source : source + 1, :], TILE),
-                one_hot(col_places_ref[source : source + 1, :], TILE),
-            )
-            place = pl.multiple_of(facts_ref[12 + source] * TILE, TILE)
-            out_ref[:, pl.ds(place, TILE)] += moved
-
-    @pl.when(jnp.logical_and(c < 2, number >= 0))
+        tile = jnp.where(s == source, mine_ref[0], other_ref[0])
+        moved = permuted(
+            tile,
+            one_hot(row_places_ref[0, source : source + 1, :], TILE),
+            one_hot(col_places_ref[source : source + 1, :], TILE),
+        )
+        half = facts_ref[4 + 4 * source + m]
+        place = pl.multiple_of(facts_ref[12 + source] * TILE, TILE)
+        out_ref[half, 0, :, pl.ds(place, TILE)] += moved
+
+    @pl.when(c < 2)
     def _():
-        panel = jnp.where(c == 0, done[:, :TILE], done[:, TILE:])
         rows = lax.broadcasted_iota(jnp.int32, (TILE, TILE), 0)
         lanes = lax.broadcasted_iota(jnp.int32, (TILE, TILE), 1)
-        keep = jnp.logical_or(number > c, jnp.logical_and(number == c, lanes <= rows))
-        out_ref[:, 0:TILE] = jnp.where(keep, panel, 0.0)
-
-    @pl.when(number < 2)
+        for half in range(2):
+            number = g + 8 * m + 32 * half
+            cut = slice(half * TILE, (half + 1) * TILE)
+            panel = jnp.where(c == 0, done[0][cut], done[1][cut])
+            keep = jnp.logical_or(number > c, jnp.logical_and(number == c, lanes <= rows))
+            out_ref[half, 0, :, 0:TILE] = jnp.where(keep, panel, 0.0)
+
+    @pl.when(jnp.logical_and(m == 0, g < 2))
     def _():
-        out_ref[:, TILE:] = jnp.zeros((TILE, TILE), F32)
-
-    @pl.when(jnp.logical_and(number < 2, c >= 2))
+        out_ref[0, 0, :, TILE:] = jnp.zeros((TILE, TILE), F32)
+
+    @pl.when(jnp.logical_and(jnp.logical_and(m == 0, g < 2), c >= 2))
     def _():
-        out_ref[:, 0:TILE] = jnp.zeros((TILE, TILE), F32)
+        out_ref[0, 0, :, 0:TILE] = jnp.zeros((TILE, TILE), F32)
 
 
 def update(facts, front_in, child_update, arrived, row_places, col_places, left, right, inverse):
     blocks = 2 * TILE // LEAF
     grid_spec = pltpu.PrefetchScalarGridSpec(
         num_scalar_prefetch=1,
-        grid=(8,),
+        grid=(4,),
         in_specs=[
-            pl.BlockSpec((TILE, 2 * TILE), lambda i, f: (i, 0)),
-            pl.BlockSpec((1, TILE, TILE), lambda i, f: (0, f[0] + 2 * (i % 4), 0)),
-            pl.BlockSpec((1, TILE, TILE), lambda i, f: (i % 4, 0, 0)),
-            pl.BlockSpec((1, 2, TILE), lambda i, f: (i % 4, 0, 0)),
-            pl.BlockSpec((2, TILE), lambda i, f: (0, 0)),
-            pl.BlockSpec((1, 4, HALF, TILE), lambda i, f: (i % 4, 0, 0, i // 4)),
-            pl.BlockSpec((4, HALF, 2 * TILE), lambda i, f: (0, 0, 0)),
-            pl.BlockSpec((blocks, LEAF, 2 * TILE), lambda i, f: (0, 0, 0)),
+            pl.BlockSpec((2, 1, TILE, 2 * TILE), lambda m, f: (0, m, 0, 0)),
+            pl.BlockSpec((1, TILE, TILE), lambda m, f: (0, f[0] + 2 * m, 0)),
+            pl.BlockSpec((1, TILE, TILE), lambda m, f: (m, 0, 0)),
+            pl.BlockSpec((1, 2, TILE), lambda m, f: (m, 0, 0)),
+            pl.BlockSpec((2, TILE), lambda m, f: (0, 0)),
+            pl.BlockSpec((1, 2, 2 * TILE, TILE), lambda m, f: (m, 0, 0, 0)),
+            pl.BlockSpec((4, HALF, 2 * TILE), lambda m, f: (0, 0, 0)),
+            pl.BlockSpec((blocks, LEAF, 2 * TILE), lambda m, f: (0, 0, 0)),
         ],
-        out_specs=pl.BlockSpec((TILE, 2 * TILE), lambda i, f: (i, 0)),
-        scratch_shapes=[
-            pltpu.VMEM((2 * TILE, 2 * TILE), BF16),
-            pltpu.VMEM((2 * TILE, 2 * TILE), BF16),
-        ],
-    )
-    return pl.pallas_call(
+        out_specs=pl.BlockSpec((2, 1, TILE, 2 * TILE), lambda m, f: (0, m, 0, 0)),
+        scratch_shapes=[pltpu.VMEM((2 * TILE, 2 * TILE), BF16)] * 4,
+    )
+    out = pl.pallas_call(
         update_kernel,
-        out_shape=jax.ShapeDtypeStruct((8 * TILE, 2 * TILE), F32),
+        out_shape=jax.ShapeDtypeStruct((2, 4, TILE, 2 * TILE), F32),
         grid_spec=grid_spec,
         compiler_params=pltpu.CompilerParams(vmem_limit_bytes=48 * 1024 * 1024),
         name="update",
-    )(facts, front_in, child_update, arrived, row_places, col_places, left, right, inverse)
+    )(
+        facts, front_in.reshape(2, 4, TILE, 2 * TILE), child_update, arrived,
+        row_places, col_places, left, right, inverse,
+    )
+    return out.reshape(8 * TILE, 2 * TILE)
 
 
 def local(front_in, child_update, child_map):

time: 138 us -> 95.4 us (0.69)
  the two profiles are of different devices: /device:TPU:158 before, /device:TPU:60 now
where the time goes in v2:
time: 95.4 us; the launch traced here: 95.2 us
  Pallas kernels  91.6 us (96%)
  local copies, waits for them, and re-layouts  2.84 us (3%)
    pallas_call x1, Pallas kernels, exchange(): pl.pallas_call(exchange_kernel, out_shape=outs, grid=(1,), in_specs=[pl.B...  78.2 us
    pallas_call x1, Pallas kernels, update(): pl.pallas_call(update_kernel, out_shape=jax.ShapeDtypeStruct((2, 4, TILE,...  13.4 us
    unnamed x4, local copies, waits for them, and re-layouts  2.45 us

profile of v2, /device:TPU:60, one launch (start us, length us, event | category | flops | bytes accessed | tf_op | source)
XLA Modules:
  0.0 95.2 jit_solution(11868018936964846110)
XLA Ops:
  0.0 0.7 multiply_add_fusion
  0.7 0.1 slice_reduce_fusion
  0.8 0.8 copy.16
  1.7 0.1 copy.8
  1.8 0.1 squeeze.16
  1.9 0.1 concatenate.3.facts_ref
  2.0 0.0 copy-start
  2.0 1.6 %copy-done = f32[1,2048,256]{2,1,0:T(8,128)S(1)} copy-done((f32[1,2048,256]{2,1,0:T(8,128)S(1)}, f32[1,2048,256]{2,1,0:T(8,128)}, u32[]{:S(2)}) %copy-start) | copy-done | bytes 2097176
  3.6 78.2 %exchange.1 = (f32[4,2,512,256]{3,2,1,0:T(8,128)}, f32[4,128,512]{2,1,0:T(8,128)S(1)}, f32[8,64,512]{2,1,0:T(8,128)S(1)}, f32[4,256,256]{2,1,0:T(8,128)S(1)}) custom-call(f32[2048,512]{1,0:T(8,128)} %front_ref.1, f32[1,2048,256]{2,1,0:T(8,128)S(1)} %copy-done, f32[1,2048,256]{2,1,0:T(8,128)S(1)} %copy-done, s32[2,256]{1,0:T(2,128)S(1)} %fusion.2.row_places_ref, ...), custom_call_target="tpu_custom_call" | custom-call | tf_op jit(solution)/shard_map/exchange/pallas_call | solution.py:440
  81.8 13.4 %update.1 = f32[2,4,256,512]{3,2,1,0:T(8,128)} custom-call(s32[14]{0:T(128)S(1)} %concatenate.3.facts_ref, f32[2,4,256,512]{3,2,1,0:T(8,128)} %bitcast.25, f32[1,2048,256]{2,1,0:T(8,128)S(1)} %copy-done, f32[4,256,256]{2,1,0:T(8,128)S(1)} %get-tuple-element.9.other_ref, s32[4,2,256]{2,1,0:T(2,128)S(1)} %fusion.row_places_ref, ...), custom_call_target="tpu_custom_call" | custom-call | tf_op jit(solution)/shard_map/update/pallas_call | solution.py:561
  (7 shorter events, 0.1 us)
Async XLA Ops:
  2.0 1.6 %copy-start = (f32[1,2048,256]{2,1,0:T(8,128)S(1)}, f32[1,2048,256]{2,1,0:T(8,128)}, u32[]{:S(2)}) copy-start(f32[1,2048,256]{2,1,0:T(8,128)} %mine_ref.1) | copy-start | bytes 6291460

commit v3 on v2

--- a/solution.py
+++ b/solution.py
@@ -105,7 +105,7 @@
 def exchange_kernel(
     front_ref, tile_ref, child_ref, row_places_ref, col_places_ref,
     left_ref, right_ref, inverse_ref, child_out_ref,
-    made, turned, early, corner, work, strip, send_sems, left_sems, right_sems, inverse_sems,
+    made, turned, early, corner, work, send_sems, left_sems, right_sems, inverse_sems,
     child_sems, corner_sems, local_sems,
 ):
     s = lax.axis_index("sub")
@@ -225,6 +225,11 @@
             [first, r == 0, c == 0],
             made.at[part, :, pl.ds(0, TILE)], corner.at[part], corner_sems.at[part],
             at(cc=1),
+        )
+        send(
+            [first, r == 1, c == 1],
+            made.at[part, :, pl.ds(0, TILE)], corner.at[2 + part], corner_sems.at[2 + part],
+            to_row(0),
         )
     def left_at(m, q):
         return left_ref.at[m, q // PARTS, pl.ds(q % PARTS * RUN, RUN), :]
@@ -272,7 +277,8 @@
         jnp.logical_not(jnp.logical_and(home, jnp.logical_and(first, r == panel)))
         for panel in range(2)
     ]
-    for q in range(2 * PARTS):
+    order = [part + PARTS * panel for part in range(PARTS) for panel in range(2)]
+    for q in order:
         await_left([source_rider, not_made[q // PARTS]], mine, q)
         pass_left([source_rider], mine, q, [to_up, to_down, to_twin])
 
@@ -313,20 +319,11 @@
 
     @pl.when(chief)
     def _():
-        for part in range(2):
+        for part in range(4):
             await_at(corner.at[part], corner_sems.at[part])
-            await_at(right_ref.at[2 + part], right_sems.at[2 + part])
-        for q in range(4):
-            pltpu.make_async_copy(
-                right_ref.at[q, :, pl.ds(0, TILE)], strip.at[q], local_sems.at[8 + q]
-            ).start()
-        for q in range(4):
-            pltpu.make_async_copy(
-                right_ref.at[q, :, pl.ds(0, TILE)], strip.at[q], local_sems.at[8 + q]
-            ).wait()
-        work[0:TILE, 0:TILE] = corner[...].reshape(TILE, TILE)
-        work[0:TILE, TILE:] = strip[0:2].reshape(TILE, TILE)
-        work[TILE:, TILE:] = strip[2:4].reshape(TILE, TILE)
+        work[0:TILE, 0:TILE] = corner[0:2].reshape(TILE, TILE)
+        work[0:TILE, TILE:] = made[:, :, 0:TILE].reshape(TILE, TILE)
+        work[TILE:, TILE:] = corner[2:4].reshape(TILE, TILE)
         work[TILE:, 0:TILE] = jnp.zeros((TILE, TILE), F32)
 
     lanes = lax.broadcasted_iota(jnp.int32, (1, 2 * TILE), 1)
@@ -389,7 +386,7 @@
     across = (mine + 2) % 4
     block_down = ((z + 7 - s) // 2) % 4
     block_up = ((z + 1 + 8 - s) // 2) % 4
-    for q in range(2 * PARTS):
+    for q in order:
         await_left([other_rider], block_down, q)
         pass_left([other_rider], block_down, q, [to_up, to_twin])
         await_left([other_rider], block_up, q)
@@ -401,7 +398,7 @@
     pass_right(rides)
     send_children((2, 3))
     far_down, far_up = (block_down + 3) % 4, (block_up + 1) % 4
-    for q in range(2 * PARTS):
+    for q in order:
         await_left([other_rider], far_down, q)
         pass_left([other_rider], far_down, q, ([to_up] if q < PARTS else []) + [to_twin])
         await_left([other_rider], far_up, q)
@@ -416,7 +413,7 @@
 
         send_inverse(b, [jnp.logical_not(chief)])
 
-    await_right(jnp.logical_not(chief))
+    await_right(always)
     for m in range(4):
         for q in range(2 * PARTS):
             await_left([jnp.logical_not(rides)], m, q)
@@ -453,15 +450,14 @@
             pltpu.VMEM((2, HALF, 2 * TILE), F32),
             pltpu.VMEM((2 * TILE, TILE), F32),
             pltpu.VMEM((TILE, TILE), F32),
-            pltpu.VMEM((2, HALF, TILE), F32),
+            pltpu.VMEM((4, HALF, TILE), F32),
             pltpu.VMEM((2 * TILE, 2 * TILE), F32),
-            pltpu.VMEM((4, HALF, TILE), F32),
             pltpu.SemaphoreType.DMA((SENDS,)),
             pltpu.SemaphoreType.DMA((4, 2 * PARTS)),
             pltpu.SemaphoreType.DMA((4,)),
             pltpu.SemaphoreType.DMA((blocks,)),
             pltpu.SemaphoreType.DMA((5,)),
-            pltpu.SemaphoreType.DMA((2,)),
+            pltpu.SemaphoreType.DMA((4,)),
             pltpu.SemaphoreType.DMA((13,)),
         ],
         compiler_params=pltpu.CompilerParams(

time: 95.4 us -> 95.4 us (level)
  no operation moved by 1% of the time
where the time goes in v3:
time: 95.4 us; the launch traced here: 95.2 us
  Pallas kernels  91.5 us (96%)
  local copies, waits for them, and re-layouts  2.84 us (3%)
    pallas_call x1, Pallas kernels, exchange(): pl.pallas_call(exchange_kernel, out_shape=outs, grid=(1,), in_specs=[pl.B...  78.2 us
    pallas_call x1, Pallas kernels, update(): pl.pallas_call(update_kernel, out_shape=jax.ShapeDtypeStruct((2, 4, TILE,...  13.3 us
    unnamed x4, local copies, waits for them, and re-layouts  2.45 us

profile of v3, /device:TPU:60, one launch (start us, length us, event | category | flops | bytes accessed | tf_op | source)
XLA Modules:
  0.0 95.2 jit_solution(4453718661989155882)
XLA Ops:
  0.0 0.7 multiply_add_fusion
  0.7 0.1 slice_reduce_fusion
  0.8 0.8 copy.16
  1.7 0.1 copy.8
  1.8 0.1 squeeze.16
  1.9 0.1 concatenate.3.facts_ref
  2.0 0.0 copy-start
  2.0 1.6 %copy-done = f32[1,2048,256]{2,1,0:T(8,128)S(1)} copy-done((f32[1,2048,256]{2,1,0:T(8,128)S(1)}, f32[1,2048,256]{2,1,0:T(8,128)}, u32[]{:S(2)}) %copy-start) | copy-done | bytes 2097176
  3.6 78.2 %exchange.1 = (f32[4,2,512,256]{3,2,1,0:T(8,128)}, f32[4,128,512]{2,1,0:T(8,128)S(1)}, f32[8,64,512]{2,1,0:T(8,128)S(1)}, f32[4,256,256]{2,1,0:T(8,128)S(1)}) custom-call(f32[2048,512]{1,0:T(8,128)} %front_ref.1, f32[1,2048,256]{2,1,0:T(8,128)S(1)} %copy-done, f32[1,2048,256]{2,1,0:T(8,128)S(1)} %copy-done, s32[2,256]{1,0:T(2,128)S(1)} %fusion.2.row_places_ref, ...), custom_call_target="tpu_custom_call" | custom-call | tf_op jit(solution)/shard_map/exchange/pallas_call | solution.py:437
  81.9 13.3 %update.1 = f32[2,4,256,512]{3,2,1,0:T(8,128)} custom-call(s32[14]{0:T(128)S(1)} %concatenate.3.facts_ref, f32[2,4,256,512]{3,2,1,0:T(8,128)} %bitcast.25, f32[1,2048,256]{2,1,0:T(8,128)S(1)} %copy-done, f32[4,256,256]{2,1,0:T(8,128)S(1)} %get-tuple-element.9.other_ref, s32[4,2,256]{2,1,0:T(2,128)S(1)} %fusion.row_places_ref, ...), custom_call_target="tpu_custom_call" | custom-call | tf_op jit(solution)/shard_map/update/pallas_call | solution.py:557
  (7 shorter events, 0.1 us)
Async XLA Ops:
  2.0 1.6 %copy-start = (f32[1,2048,256]{2,1,0:T(8,128)S(1)}, f32[1,2048,256]{2,1,0:T(8,128)}, u32[]{:S(2)}) copy-start(f32[1,2048,256]{2,1,0:T(8,128)} %mine_ref.1) | copy-start | bytes 6291460
